TPU v7x, 32 devices: a whole 2x2x4 slice. The times are simulated.
32 devices in a mesh: dp: 4 (over x, core), tensor: 8 (over z, y).
Axes of the slice: x: 2, y: 2, z: 4, core: 2. Of those that a mesh axis runs over, the one named last changes fastest.
Arguments:
- stream: bfloat16 [1536, 2560], P(('dp', 'tensor')), may hold values from -26 to 26
- lengths: int32 [4, 6], P('dp'), may hold values from 16 to 192, as said below
- page_table: int32 [96], P('dp'), may hold values from 0 to 95, as said below
- request_prompt: int32 [64], P('dp'), may hold values from 0 to 23
- attn_gain: bfloat16 [2560], replicated, may hold values from 0.099609375 to 1.8984375
- query_gain: bfloat16 [128], replicated, may hold values from 0.5 to 10, as said below
- key_gain: bfloat16 [128], replicated, may hold values from 0.5 to 10, as said below
- mlp_gain: bfloat16 [2560], replicated, may hold values from 0.099609375 to 1.8984375
- w_query: bfloat16 [2560, 4096], P(None, 'tensor'), may hold values from -0.125 to 0.125
- key_value_weight: bfloat16 [2560, 2048], P(None, 'tensor'), may hold values from -0.125 to 0.125
- w_out: bfloat16 [4096, 2560], P('tensor'), may hold values from -0.5 to 0.5
- w_gate: bfloat16 [2560, 9728], P(None, 'tensor'), may hold values from -0.125 to 0.125
- w_up: bfloat16 [2560, 9728], P(None, 'tensor'), may hold values from -0.125 to 0.125
- w_down: bfloat16 [9728, 2560], P('tensor'), may hold values from -0.0625 to 0.0625
Outputs:
- layer_out: bfloat16 [1536, 2560], P(('dp', 'tensor'))
- paged_key_value_cache: bfloat16 [96, 16, 2048], P('dp', None, 'tensor')
- request_state: bfloat16 [64, 2560], P('dp', 'tensor')
Inputs may be any that keep to these rules, and one draw needn't show every extreme that they name: Every length is a multiple of 16; each batch's lengths add up to 384, and the largest length of each batch is exactly 192. page_table is a permutation of all global slots; slot v belongs to owner v // 24, and each batch writes exactly 6 pages to each owner. `query_gain`: positive gains. `key_gain`: positive gains.
All inputs are finite; a program needn't handle non-finite values.
Results may differ from a plain program's by a relative error of at most 0.02.
The roundings to bfloat16 on the way count: a program that leaves them out, or rounds other values in their place, can miss the bound.
Values may be sent and summed in bfloat16 or wider, within the bound.
A program may use at most 128 MiB of HBM per device.

v0:
```python
import math

import jax
import jax.numpy as jnp
from jax import lax
from jax.sharding import PartitionSpec as P

KEY_VALUE_HEADS = 8
HEAD_SIZE = 128
PAGE_TOKENS = 16


epsilon = 1e-06
rope_base = 1000000.0


def partner_2(value, axis, bit):
    mask = 2**bit
    pairs = [(source, source ^ mask) for source in range(lax.axis_size(axis))]
    return lax.ppermute(value, axis, pairs)


def row_norm(inputs, gain):
    inputs = inputs.astype(jnp.float32)
    scale = lax.rsqrt(jnp.mean(inputs * inputs, axis=-1, keepdims=True) + epsilon)
    return inputs * scale * gain.astype(jnp.float32)


def rotate(inputs, position):
    half_dim = inputs.shape[-1] // 2
    frequency = rope_base ** (-2.0 * jnp.arange(half_dim, dtype=jnp.float32) / inputs.shape[-1])
    angles = position.astype(jnp.float32)[:, None] * frequency[None, :]
    cosine = jnp.cos(angles)[:, None, :]
    sine_part = jnp.sin(angles)[:, None, :]
    front = inputs[..., :half_dim]
    second = inputs[..., half_dim:]
    return jnp.concatenate(
        [front * cosine - second * sine_part, second * cosine + front * sine_part], axis=-1
    )


def prompt_layout(lengths_row, token_count):
    prompt_ends = jnp.cumsum(lengths_row)
    prompt_starts = prompt_ends - lengths_row
    row_ids = jnp.arange(token_count, dtype=jnp.int32)
    prompt = jnp.sum((row_ids[:, None] >= prompt_ends[None, :]).astype(jnp.int32), axis=1)
    inside = (row_ids[:, None] >= prompt_starts[None, :]) & (
        row_ids[:, None] < prompt_ends[None, :]
    )
    offset = jnp.sum(jnp.where(inside, prompt_starts[None, :], 0), axis=1)
    return (prompt, row_ids - offset, prompt_starts, prompt_ends)


def per_device(
    stream,
    lengths,
    page_table,
    request_prompt,
    attn_gain,
    query_gain,
    key_gain,
    mlp_gain,
    w_query,
    key_value_weight,
    w_out,
    w_gate,
    w_up,
    w_down,
):
    tok_dev = stream.shape[0]
    tensor_element_count = lax.axis_size("tensor")
    token_count = tok_dev * tensor_element_count
    my_index = lax.axis_index("tensor")
    heads_dev = w_query.shape[1] // HEAD_SIZE
    query_cols = heads_dev * HEAD_SIZE
    prompt, position, prompt_starts, prompt_ends = prompt_layout(lengths[0], token_count)
    portion = lax.all_gather(
        row_norm(stream, attn_gain).astype(jnp.bfloat16), "tensor", axis=0, tiled=True
    )
    joined = jnp.concatenate(
        [
            jnp.dot(portion, w_query, preferred_element_type=jnp.float32),
            jnp.dot(portion, key_value_weight, preferred_element_type=jnp.float32),
        ],
        axis=1,
    )
    queries = joined[:, :query_cols].reshape(token_count, heads_dev, HEAD_SIZE)
    kv_part = joined[:, query_cols:].astype(jnp.bfloat16)
    key_value_group = tensor_element_count // KEY_VALUE_HEADS
    for bit_id in range(key_value_group.bit_length() - 1):
        partner = partner_2(kv_part, "tensor", bit_id)
        upper_half = my_index // 2**bit_id % 2
        kv_part = jnp.where(
            upper_half == 1,
            jnp.concatenate([partner, kv_part], axis=1),
            jnp.concatenate([kv_part, partner], axis=1),
        )
    key_flat = rotate(row_norm(kv_part[:, None, :HEAD_SIZE], key_gain), position).astype(
        jnp.bfloat16
    )[:, 0, :]
    value_matrix_rows = kv_part[:, HEAD_SIZE:]
    q_rot = rotate(row_norm(queries, query_gain), position).astype(jnp.bfloat16)
    piece_cols = key_value_weight.shape[1]
    head_rows = jnp.concatenate([key_flat, value_matrix_rows], axis=1)
    own_cols = lax.dynamic_slice_in_dim(
        head_rows, my_index % key_value_group * piece_cols, piece_cols, 1
    )
    page_count = token_count // PAGE_TOKENS
    page_rows = own_cols.reshape(page_count, PAGE_TOKENS, piece_cols)
    group_count = lax.axis_size("dp")
    capacity = page_count // group_count
    owners = page_table // page_count
    slot_ids = page_table % page_count
    hits = (owners[:, None] == jnp.arange(group_count, dtype=jnp.int32)[None, :]).astype(jnp.int32)
    order_in = jnp.sum((jnp.cumsum(hits, axis=0) - hits) * hits, axis=1)
    buffer_pos = owners * capacity + order_in
    source = (
        jnp.zeros((page_count,), jnp.int32)
        .at[buffer_pos]
        .set(jnp.arange(page_count, dtype=jnp.int32))
    )
    send_pages = page_rows[source].reshape(group_count, capacity, PAGE_TOKENS, piece_cols)
    send_slots = slot_ids[source].reshape(group_count, capacity)
    got_pages, got_slots = (
        lax.all_to_all(send_pages, "dp", split_axis=0, concat_axis=0, tiled=True),
        lax.all_to_all(send_slots, "dp", split_axis=0, concat_axis=0, tiled=True),
    )
    paged_key_value_cache = (
        jnp.zeros((page_count, PAGE_TOKENS, piece_cols), jnp.bfloat16)
        .at[got_slots.reshape(-1)]
        .set(got_pages.reshape(page_count, PAGE_TOKENS, piece_cols))
    )
    block_rows = min(512, token_count)
    block_total = token_count // block_rows
    score_scale = math.sqrt(HEAD_SIZE)
    all_ids = jnp.arange(token_count, dtype=jnp.int32)
    local_ids = jnp.arange(block_rows, dtype=jnp.int32)

    def dense_block(block_index):
        first_row = block_index * block_rows
        q_block = lax.dynamic_slice_in_dim(q_rot, first_row, block_rows, 0)
        q_prompt = lax.dynamic_slice_in_dim(prompt, first_row, block_rows, 0)
        row_ids = first_row + local_ids
        scores = (
            jnp.einsum("qhd,kd->hqk", q_block, key_flat, preferred_element_type=jnp.float32)
            / score_scale
        )
        allowed = ((q_prompt[:, None] == prompt[None, :]) & (row_ids[:, None] >= all_ids[None, :]))[
            None
        ]
        peak = jnp.max(jnp.where(allowed, scores, -jnp.inf), axis=2, keepdims=True)
        weight = jnp.where(allowed, jnp.exp(scores - peak), 0.0)
        total_weight = jnp.sum(weight, axis=2, keepdims=True)
        running = jnp.einsum(
            "hqk,kd->hqd",
            weight.astype(jnp.bfloat16),
            value_matrix_rows,
            preferred_element_type=jnp.float32,
        )
        return (running / total_weight).astype(jnp.bfloat16)

    block_ids = jnp.arange(block_total, dtype=jnp.int32)
    blocks_out = lax.map(dense_block, block_ids)
    attn = jnp.transpose(blocks_out, (0, 2, 1, 3)).reshape(token_count, query_cols)
    attn_sum = lax.psum_scatter(
        jnp.dot(attn, w_out, preferred_element_type=jnp.float32).astype(jnp.bfloat16),
        "tensor",
        scatter_dimension=0,
        tiled=True,
    ).astype(jnp.float32)
    resid = (stream.astype(jnp.float32) + attn_sum).astype(jnp.bfloat16)
    portion = lax.all_gather(
        row_norm(resid, mlp_gain).astype(jnp.bfloat16), "tensor", axis=0, tiled=True
    )
    gate_rows = jnp.dot(portion, w_gate, preferred_element_type=jnp.float32)
    upward = jnp.dot(portion, w_up, preferred_element_type=jnp.float32)
    hidden = (jax.nn.silu(gate_rows) * upward).astype(jnp.bfloat16)
    mlp_sum = lax.psum_scatter(
        jnp.dot(hidden, w_down, preferred_element_type=jnp.float32).astype(jnp.bfloat16),
        "tensor",
        scatter_dimension=0,
        tiled=True,
    ).astype(jnp.float32)
    layer_out = (resid.astype(jnp.float32) + mlp_sum).astype(jnp.bfloat16)
    my_rows = my_index * tok_dev + jnp.arange(tok_dev, dtype=jnp.int32)
    select = ((prompt_ends - 1)[:, None] == my_rows[None, :]).astype(jnp.bfloat16)
    end_terms = jnp.dot(select, layer_out, preferred_element_type=jnp.float32)
    end_rows = lax.psum_scatter(
        end_terms.astype(jnp.bfloat16), "tensor", scatter_dimension=1, tiled=True
    )
    table = lax.all_gather(end_rows, "dp", axis=0, tiled=True)
    pick = (request_prompt[:, None] == jnp.arange(table.shape[0], dtype=jnp.int32)[None, :]).astype(
        jnp.bfloat16
    )
    request_state = jnp.dot(pick, table, preferred_element_type=jnp.float32).astype(jnp.bfloat16)
    return (layer_out, paged_key_value_cache, request_state)


def solution(mesh):
    placed = (
        P(("dp", "tensor"), None),
        P("dp", None),
        P("dp"),
        P("dp"),
        P(),
        P(),
        P(),
        P(),
        P(None, "tensor"),
        P(None, "tensor"),
        P("tensor", None),
        P(None, "tensor"),
        P(None, "tensor"),
        P("tensor", None),
    )
    return jax.shard_map(
        per_device,
        mesh=mesh,
        in_specs=placed,
        out_specs=(P(("dp", "tensor"), None), P("dp", None, "tensor"), P("dp", "tensor")),
        check_vma=False,
    )
```

profile of v0, /device:TPU:0, one launch (start us, length us, event | category | flops | bytes accessed | tf_op | source)
XLA Modules:
  0.0 365.6 jit_solution(2273115526215917327)
XLA Ops:
  7.2 1.2 fusion.13
  9.2 1.8 fusion.15
  14.7 1.5 multiply_cosine_fusion
  16.3 45.1 %all-gather.4.cloned.1.call-done = bf16[384,2560]{1,0:T(8,128)(2,1)} async-done(((bf16[48,2560]{1,0:T(8,128)(2,1)}), bf16[384,2560]{1,0:T(8,128)(2,1)}) %all-gather.4.cloned.1.call-update) | async-done | bytes 1966096 | tf_op jit(solution)/shard_map/all_gather | solution.py:77
  61.4 2.9 convolution_convert_fusion.3
  65.0 2.7 fusion.60
  67.7 1.1 reshape.301
  68.9 2.3 multiply_reduce_fusion
  71.2 1.0 copy.43
  72.5 1.4 subtract_convert_fusion
  74.5 1.4 copy-done.2
  75.9 1.0 fusion.59
  76.9 4.2 %fusion.6 = bf16[4,384,128]{1,2,0:T(8,128)(2,1)} fusion(f32[4,384]{1,0:T(4,128)S(1)} %fusion.59, f32[384,384,4]{1,0,2:T(8,128)} %copy-done.2, pred[384,384]{0,1:T(8,128)(4,1)S(1)} %copy-done.8, bf16[384,256]{0,1:T(8,128)(2,1)S(1)} %copy-done.7), kind=kOutput, calls=%fused_computation.17 | convolution fusion | flops 154929024 | bytes 5511168 | tf_op jit(solution)/shard_map/while/body/eval_jaxpr/hqk,kd->hqd/dot_general | solution.py:154
  81.0 3.5 convolution_convert_fusion.1
  84.6 66.4 %reduce-scatter.6.cloned.1.call-done = bf16[48,2560]{1,0:T(8,128)(2,1)} async-done(((bf16[384,2560]{1,0:T(8,128)(2,1)}), bf16[48,2560]{1,0:T(8,128)(2,1)}) %reduce-scatter.6.cloned.1.call-update) | async-done | bytes 245776 | tf_op jit(solution)/shard_map/reduce_scatter | solution.py:165
  151.1 1.1 fusion.17
  152.2 1.8 fusion.19
  154.2 46.3 %all-gather.6.cloned.1.call-done = bf16[384,2560]{1,0:T(8,128)(2,1)} async-done(((bf16[48,2560]{1,0:T(8,128)(2,1)}), bf16[384,2560]{1,0:T(8,128)(2,1)}) %all-gather.6.cloned.1.call-update) | async-done | bytes 1966096 | tf_op jit(solution)/shard_map/all_gather | solution.py:172
  200.5 8.1 %fusion.61 = f32[384,1216]{0,1:T(8,128)} fusion(bf16[384,2560]{1,0:T(8,128)(2,1)} %all-gather.6.cloned.1.call-done, bf16[2560,1216]{0,1:T(8,128)(2,1)} %param.25), kind=kOutput, calls=%fused_computation.114 | convolution fusion | flops 2390753280 | bytes 10059776 | tf_op jit(solution)/shard_map/dot_general | solution.py:175
  208.6 13.0 %convolution_convert_fusion = bf16[384,2560]{1,0:T(8,128)(2,1)} fusion(bf16[1216,2560]{1,0:T(8,128)(2,1)} %param.27, bf16[384,2560]{1,0:T(8,128)(2,1)} %all-gather.6.cloned.1.call-done, bf16[2560,1216]{0,1:T(8,128)(2,1)} %param.26, f32[384,1216]{0,1:T(8,128)} %fusion.61), kind=kOutput, calls=%fused_computation.5 | convolution fusion | flops 4785291264 | bytes 18251776 | tf_op jit(solution)/shard_map/dot_general | solution.py:179
  224.0 3.2 all-to-all-start
  227.3 3.6 all-to-all-done
  233.8 1.1 pad_maximum_fusion
  234.9 1.2 gather_fusion.1
  236.1 4.0 %all-to-all-start.1 = ((bf16[4,6,16,256]{3,2,1,0:T(8,128)(2,1)}), bf16[4,6,16,256]{3,2,1,0:T(8,128)(2,1)}, u32[]{:S(2)}, u32[]{:S(2)}) async-start(bf16[4,6,16,256]{3,2,1,0:T(8,128)(2,1)} %bitcast.18), calls=%async_computation.3 | async-start | bytes 393216 | tf_op jit(solution)/shard_map/all_to_all | solution.py:125
  240.2 48.0 %reduce-scatter.8.cloned.1.call-done = bf16[48,2560]{1,0:T(8,128)(2,1)} async-done(((bf16[384,2560]{1,0:T(8,128)(2,1)}), bf16[48,2560]{1,0:T(8,128)(2,1)}) %reduce-scatter.8.cloned.1.call-update) | async-done | bytes 245776 | tf_op jit(solution)/shard_map/reduce_scatter | solution.py:178
  288.1 1.0 fusion.20
  289.4 1.2 copy.54
  290.6 2.8 scatter_fusion
  293.4 58.6 %reduce-scatter.10.cloned.1.call-done = bf16[320,6]{1,0:T(8,128)(2,1)} async-done(((bf16[2560,6]{1,0:T(8,128)(2,1)}), bf16[320,6]{1,0:T(8,128)(2,1)}) %reduce-scatter.10.cloned.1.call-update) | async-done | bytes 3856
  352.0 1.0 copy.55
  353.0 5.2 %all-gather = bf16[4,6,320]{2,1,0:T(8,128)(2,1)S(1)} all-gather(bf16[1,6,320]{2,1,0:T(8,128)(2,1)S(1)} %bitcast.87), channel_id=1, replica_groups=mesh['dp'=4,'tensor'=8] {'dp'}, dimensions={0}, use_global_device_ids=true | all-gather | bytes 19200 | tf_op jit(solution)/shard_map/all_gather | solution.py:191
  (81 shorter events, 12.8 us)
Async XLA Ops:
  7.2 73.9 %copy-start = (bf16[512,2560]{1,0:T(8,128)(2,1)S(1)}, bf16[512,2560]{1,0:T(8,128)(2,1)}, u32[]{:S(2)}) copy-start(bf16[512,2560]{1,0:T(8,128)(2,1)} %param.24) | copy-start | bytes 7864324
  7.2 54.2 %all-gather.4.cloned.1.call-start = ((), (), s32[]{:S(2)}) async-start(), calls=%async_computation.5 | async-start | bytes 2211840 | tf_op jit(solution)/shard_map/all_gather | solution.py:77
  11.0 140.1 %reduce-scatter.6.cloned.1.call-start = ((), (), s32[]{:S(2)}) async-start(), calls=%async_computation.6 | async-start | bytes 2211840 | tf_op jit(solution)/shard_map/reduce_scatter | solution.py:165
  61.4 3.6 copy-start.10
  64.3 0.7 copy-start.6
  72.5 3.4 copy-start.8
  74.5 1.4 copy-start.2
  75.9 1.0 copy-start.7
  81.0 3.6 copy-start.9
  81.0 70.0 %copy-start.1 = (bf16[48,2560]{1,0:T(8,128)(2,1)S(1)}, bf16[48,2560]{1,0:T(8,128)(2,1)}, u32[]{:S(2)}) copy-start(bf16[48,2560]{1,0:T(8,128)(2,1)} %param.14) | copy-start | bytes 737284
  84.6 115.9 %all-gather.6.cloned.1.call-start = ((), (), s32[]{:S(2)}) async-start(), calls=%async_computation.7 | async-start | bytes 2211840 | tf_op jit(solution)/shard_map/all_gather | solution.py:172
  154.0 134.2 %reduce-scatter.8.cloned.1.call-start = ((), (), s32[]{:S(2)}) async-start(), calls=%async_computation.8 | async-start | bytes 2211840 | tf_op jit(solution)/shard_map/reduce_scatter | solution.py:178
  208.6 13.0 %copy-start.11 = (s32[24]{0:T(128)S(1)}, s32[24]{0:T(128)}, u32[]{:S(2)}) copy-start(s32[24]{0:T(128)} %param.16) | copy-start | bytes 292
  221.6 12.1 %slice-start = ((bf16[384,256]{0,1:T(8,128)(2,1)}), bf16[384,128]{0,1:T(8,128)(2,1)S(1)}, s32[]{:S(2)}) async-start(bf16[384,256]{0,1:T(8,128)(2,1)} %copy-done.6), calls=%async_computation.10 | async-start | bytes 196608 | tf_op jit(solution)/shard_map/slice | solution.py:101
  221.6 66.6 %copy-start.3 = (bf16[48,2560]{1,0:T(8,128)(2,1)S(1)}, bf16[48,2560]{1,0:T(8,128)(2,1)}, u32[]{:S(2)}) copy-start(bf16[48,2560]{1,0:T(8,128)(2,1)} %reduce-scatter.6.cloned.1.call-done) | copy-start | bytes 737284
  224.0 6.9 %all-to-all-start = ((s32[4,1,6]{2,1,0:T(1,128)}), s32[4,1,6]{2,1,0:T(1,128)S(1)}, u32[]{:S(2)}, u32[]{:S(2)}) async-start(s32[4,1,6]{2,1,0:T(1,128)} %bitcast.13), calls=%async_computation.2 | async-start | bytes 4096 | tf_op jit(solution)/shard_map/all_to_all | solution.py:126
  233.8 124.4 %copy-start.12 = (s32[16]{0:T(128)S(1)}, s32[16]{0:T(128)}, u32[]{:S(2)}) copy-start(s32[16]{0:T(128)} %param.17) | copy-start | bytes 196
  236.1 54.5 %all-to-all-start.1 = ((bf16[4,6,16,256]{3,2,1,0:T(8,128)(2,1)}), bf16[4,6,16,256]{3,2,1,0:T(8,128)(2,1)}, u32[]{:S(2)}, u32[]{:S(2)}) async-start(bf16[4,6,16,256]{3,2,1,0:T(8,128)(2,1)} %bitcast.18), calls=%async_computation.3 | async-start | bytes 393216 | tf_op jit(solution)/shard_map/all_to_all | solution.py:125
  240.1 111.9 %reduce-scatter.10.cloned.1.call-start = ((), (), s32[]{:S(2)}) async-start(), calls=%async_computation.9 | async-start | bytes 737280
  289.2 69.8 %copy-start.4 = (bf16[48,2560]{1,0:T(8,128)(2,1)}, bf16[48,2560]{1,0:T(8,128)(2,1)S(1)}, u32[]{:S(2)}) copy-start(bf16[48,2560]{1,0:T(8,128)(2,1)S(1)} %fusion.20) | copy-start | bytes 737284
  293.4 65.6 %copy-start.5 = (bf16[24,16,256]{2,1,0:T(8,128)(2,1)}, bf16[24,16,256]{2,1,0:T(8,128)(2,1)S(1)}, u32[]{:S(2)}) copy-start(bf16[24,16,256]{2,1,0:T(8,128)(2,1)S(1)} %scatter_fusion) | copy-start | bytes 589828
Sparse Core Ops, SparseCore 0:
  11.1 50.2 all-gather.3
  84.7 66.3 reduce-scatter.5
  154.1 46.3 all-gather.5
  221.7 66.3 reduce-scatter.7
  291.3 60.7 reduce-scatter.9
where the time goes:
time: 366 us
  waiting for transfers between devices  268 us (73%)
  matrix products  36 us (10%)
  other arithmetic  20.5 us (6%)
  local copies, waits for them, and re-layouts  14.1 us (4%)
  between operations  14.1 us (4%)
  starting transfers between devices  7.6 us (2%)
  blocking collectives  5.2 us (1%)
    reduce_scatter x1, waiting for transfers between devices, per_device(): lax.psum_scatter(jnp.dot(attn, w_out, preferred_element_type=jnp.float32)...  66.4 us
    unnamed x6, waiting for transfers between devices  58.7 us
    reduce_scatter x1, waiting for transfers between devices, per_device(): lax.psum_scatter(jnp.dot(hidden, w_down, preferred_element_type=jnp.float...  48 us
    all_gather x1, waiting for transfers between devices, per_device(): lax.all_gather(row_norm(resid, mlp_gain).astype(jnp.bfloat16), 'tensor',...  46.3 us
    all_gather x1, waiting for transfers between devices, per_device(): lax.all_gather(row_norm(stream, attn_gain).astype(jnp.bfloat16), 'tensor'...  45.1 us
    dot_general x1, matrix products, per_device(): jnp.dot(hidden, w_down, preferred_element_type=jnp.float32)  13 us
    dot_general x1, matrix products, per_device(): gate_rows = jnp.dot(portion, w_gate, preferred_element_type=jnp.float32)  8.08 us
  transfers between devices with their start and end apart: 7, of which 6 were waited for; matrix products, arithmetic and copies ran while one was open for 5% of the time, Pallas kernels for 0%

commit v1 on v0

--- a/solution.py
+++ b/solution.py
@@ -3,11 +3,14 @@
 import jax
 import jax.numpy as jnp
 from jax import lax
+from jax.experimental import pallas as pl
+from jax.experimental.pallas import tpu as pltpu
 from jax.sharding import PartitionSpec as P
 
 KEY_VALUE_HEADS = 8
 HEAD_SIZE = 128
 PAGE_TOKENS = 16
+MESH = pl.DeviceIdType.MESH
 
 
 epsilon = 1e-06
@@ -196,6 +199,522 @@
     return (layer_out, paged_key_value_cache, request_state)
 
 
+def fused_kernel(
+    lengths_ref,
+    stream_ref,
+    slots_ref,
+    request_ref,
+    attn_gain_ref,
+    query_gain_ref,
+    key_gain_ref,
+    mlp_gain_ref,
+    frequency_ref,
+    wq_hbm,
+    wkv_hbm,
+    wo_hbm,
+    wg_hbm,
+    wu_hbm,
+    wd_hbm,
+    layer_ref,
+    cache_ref,
+    state_ref,
+    wq,
+    wkv,
+    wo,
+    wg,
+    wu,
+    wd,
+    gathered,
+    q_rot,
+    kv_all,
+    slots_all,
+    attn,
+    hidden,
+    part,
+    y_in,
+    z_out,
+    z_in,
+    cosine,
+    sine,
+    starts,
+    resid,
+    end_out,
+    end_in,
+    table,
+    weight_sem,
+    ag_recv,
+    ag_zsend,
+    ag_ysend,
+    rs_yrecv,
+    rs_ysend,
+    rs_zrecv,
+    rs_zsend,
+    kv_send,
+    kv_recv,
+    slots_send,
+    slots_recv,
+    end_send,
+    end_recv,
+    table_send,
+    table_recv,
+):
+    f32 = jnp.float32
+    bf16 = jnp.bfloat16
+    t = lax.axis_index("tensor")
+    g = lax.axis_index("dp")
+    z = t // 2
+    y = t % 2
+    rows = stream_ref.shape[0]
+    width = stream_ref.shape[1]
+    tokens = rows * 8
+
+    pairs = ((wq_hbm, wq), (wkv_hbm, wkv), (wo_hbm, wo), (wg_hbm, wg), (wu_hbm, wu), (wd_hbm, wd))
+    loads = [
+        pltpu.make_async_copy(source, target, weight_sem.at[k])
+        for k, (source, target) in enumerate(pairs)
+    ]
+    for load in loads:
+        load.start()
+
+    barrier = pltpu.get_barrier_semaphore()
+    for k in range(1, 8):
+        pl.semaphore_signal(barrier, inc=1, device_id=(g, (t + k) % 8), device_id_type=MESH)
+    for k in range(1, 4):
+        pl.semaphore_signal(barrier, inc=1, device_id=((g + k) % 4, t), device_id_type=MESH)
+
+    def normed(value, gain_ref):
+        scale = lax.rsqrt(jnp.mean(value * value, axis=-1, keepdims=True) + epsilon)
+        return value * scale * gain_ref[...].astype(f32)
+
+    gathered[0, t] = normed(stream_ref[...].astype(f32), attn_gain_ref).astype(bf16)
+    pl.semaphore_wait(barrier, 10)
+
+    def y_copy(source, target, send, recv):
+        return pltpu.make_async_remote_copy(
+            src_ref=source, dst_ref=target, send_sem=send, recv_sem=recv,
+            device_id=(g, z * 2 + 1 - y), device_id_type=MESH)
+
+    def z_copy(source, target, send, recv, step):
+        return pltpu.make_async_remote_copy(
+            src_ref=source, dst_ref=target, send_sem=send, recv_sem=recv,
+            device_id=(g, (z + step) * 2 + y), device_id_type=MESH)
+
+    def gather(phase, before, process):
+        def up(s):
+            slot = (z - s) * 2 + y
+            return z_copy(gathered.at[phase, slot], gathered.at[phase, slot],
+                          ag_zsend.at[phase, 0, s], ag_recv.at[phase, slot], 1)
+
+        def down(s):
+            slot = (z + s) * 2 + y
+            return z_copy(gathered.at[phase, slot], gathered.at[phase, slot],
+                          ag_zsend.at[phase, 1, s], ag_recv.at[phase, slot], -1)
+
+        def across(level):
+            slot = level * 2 + y
+            return y_copy(gathered.at[phase, slot], gathered.at[phase, slot],
+                          ag_ysend.at[phase, level], ag_recv.at[phase, slot])
+
+        def arrived(slot):
+            y_copy(gathered.at[phase, slot], gathered.at[phase, slot],
+                   ag_ysend.at[phase, 0], ag_recv.at[phase, slot]).wait_recv()
+
+        def group(level):
+            arrived(level * 2 + 1 - y)
+            process(level)
+
+        def groups(s):
+            if s == 0:
+                group(z)
+            else:
+                pl.when(z - s >= 0)(lambda: group(z - s))
+                pl.when(z + s <= 3)(lambda: group(z + s))
+
+        for s in range(4):
+            if s:
+                @pl.when(z - s >= 0)
+                def _():
+                    arrived((z - s) * 2 + y)
+
+                    @pl.when(z < 3)
+                    def _():
+                        up(s).start()
+
+                    across(z - s).start()
+
+                @pl.when(z + s <= 3)
+                def _():
+                    arrived((z + s) * 2 + y)
+
+                    @pl.when(z > 0)
+                    def _():
+                        down(s).start()
+
+                    across(z + s).start()
+
+                groups(s - 1)
+            else:
+                pl.when(z < 3)(lambda: up(0).start())
+                pl.when(z > 0)(lambda: down(0).start())
+                across(z).start()
+                before()
+        groups(3)
+
+        for s in range(4):
+            pl.when((z - s >= 0) & (z < 3))(lambda: up(s).wait_send())
+            pl.when((z + s <= 3) & (z > 0))(lambda: down(s).wait_send())
+            across(s).wait_send()
+
+    packed = 27 + 72 * z - 15 * (z * (z - 1) // 2) + 5 * (z * (z - 1) * (z - 2))
+    order = [packed % 4, packed // 4 % 4, packed // 16 % 4, packed // 64]
+
+    def send_part(phase, level):
+        return y_copy(part.at[phase, level, 1 - y], y_in.at[phase, level],
+                      rs_ysend.at[phase, level], rs_yrecv.at[phase, level])
+
+    def flow(phase, level, direction, step):
+        return z_copy(z_out.at[phase, level], z_in.at[phase, direction, level],
+                      rs_zsend.at[phase, level], rs_zrecv.at[phase, direction, level], step)
+
+    def scatter(phase):
+        for i in range(3):
+            level = order[i]
+            send_part(phase, level).wait_recv()
+
+            @pl.when(level > z)
+            def _():
+                total = part[phase, level, y].astype(f32) + y_in[phase, level].astype(f32)
+
+                @pl.when(z > 0)
+                def _():
+                    flow(phase, level, 0, 1).wait_recv()
+                    z_out[phase, level] = (total + z_in[phase, 0, level].astype(f32)).astype(bf16)
+
+                @pl.when(z == 0)
+                def _():
+                    z_out[phase, level] = total.astype(bf16)
+
+                flow(phase, level, 0, 1).start()
+
+            @pl.when(level < z)
+            def _():
+                total = part[phase, level, y].astype(f32) + y_in[phase, level].astype(f32)
+
+                @pl.when(z < 3)
+                def _():
+                    flow(phase, level, 1, -1).wait_recv()
+                    z_out[phase, level] = (total + z_in[phase, 1, level].astype(f32)).astype(bf16)
+
+                @pl.when(z == 3)
+                def _():
+                    z_out[phase, level] = total.astype(bf16)
+
+                flow(phase, level, 1, -1).start()
+
+        send_part(phase, z).wait_recv()
+        resid[1] = part[phase, z, y].astype(f32) + y_in[phase, z].astype(f32)
+
+        @pl.when(z > 0)
+        def _():
+            flow(phase, z, 0, 1).wait_recv()
+            resid[1] = resid[1] + z_in[phase, 0, z].astype(f32)
+
+        @pl.when(z < 3)
+        def _():
+            flow(phase, z, 1, -1).wait_recv()
+            resid[1] = resid[1] + z_in[phase, 1, z].astype(f32)
+
+        for level in range(4):
+            send_part(phase, level).wait_send()
+            pl.when(z != level)(lambda: flow(phase, level, 0, 1).wait_send())
+        return resid[1]
+
+    def angles():
+        ids = lax.broadcasted_iota(jnp.int32, (tokens, HEAD_SIZE), 0)
+        begin = jnp.int32(0)
+        offset = jnp.zeros((tokens, HEAD_SIZE), jnp.int32)
+        for k in range(lengths_ref.shape[1]):
+            end = begin + lengths_ref[0, k]
+            offset = jnp.where((ids >= begin) & (ids < end), begin, offset)
+            begin = end
+        starts[...] = offset
+        angle = (ids - offset).astype(f32) * frequency_ref[...]
+        lane = lax.broadcasted_iota(jnp.int32, (tokens, HEAD_SIZE), 1)
+        cosine[...] = jnp.cos(angle)
+        signed = jnp.sin(angle)
+        sine[...] = jnp.where(lane < HEAD_SIZE // 2, -signed, signed)
+        slots_all[0] = slots_ref[...]
+        loads[0].wait()
+        loads[1].wait()
+
+    heads = wq.shape[1] // HEAD_SIZE
+
+    def project(level):
+        inputs = gathered[0, pl.ds(level * 2, 2)].reshape(2 * rows, width)
+        span = pl.ds(pl.multiple_of(level * 2 * rows, 32), 2 * rows)
+        cos_rows = cosine[span, :]
+        sin_rows = sine[span, :]
+
+        def rotated(value):
+            return value * cos_rows + pltpu.roll(value, HEAD_SIZE // 2, 1) * sin_rows
+
+        for pair in range(heads // 2):
+            block = jnp.dot(inputs, wq[:, pair * 256:(pair + 1) * 256], preferred_element_type=f32)
+            for k in range(2):
+                head = block[:, k * HEAD_SIZE:(k + 1) * HEAD_SIZE]
+                q_rot[pair * 2 + k, span, :] = rotated(normed(head, query_gain_ref)).astype(bf16)
+        keyval = jnp.dot(inputs, wkv[...], preferred_element_type=f32).astype(bf16)
+        key_head = keyval[:, :HEAD_SIZE].astype(f32)
+        kv_all[0, span, :HEAD_SIZE] = rotated(normed(key_head, key_gain_ref)).astype(bf16)
+        kv_all[0, span, HEAD_SIZE:] = keyval[:, HEAD_SIZE:]
+
+    gather(0, angles, project)
+
+    def kv_copies(k):
+        peer = (lax.rem(g + k, 4), t)
+        return (
+            pltpu.make_async_remote_copy(
+                src_ref=kv_all.at[0], dst_ref=kv_all.at[k], send_sem=kv_send.at[k],
+                recv_sem=kv_recv.at[k], device_id=peer, device_id_type=MESH),
+            pltpu.make_async_remote_copy(
+                src_ref=slots_all.at[0], dst_ref=slots_all.at[k], send_sem=slots_send.at[k],
+                recv_sem=slots_recv.at[k], device_id=peer, device_id_type=MESH),
+        )
+
+    for k in range(1, 4):
+        for copy in kv_copies(k):
+            copy.start()
+
+    block = 128
+    for q_block in range(tokens // block):
+        span = q_block * block
+        keys = span + block
+        row_id = span + lax.broadcasted_iota(jnp.int32, (block, keys), 0)
+        key_id = lax.broadcasted_iota(jnp.int32, (block, keys), 1)
+        first = jnp.concatenate([starts[span:keys, :]] * (keys // block), axis=1)
+        allowed = (key_id >= first) & (key_id <= row_id)
+        key_rows = kv_all[0, :keys, :HEAD_SIZE]
+        value_rows = kv_all[0, :keys, HEAD_SIZE:]
+        for head in range(heads):
+            scores = lax.dot_general(
+                q_rot[head, span:keys, :], key_rows, (((1,), (1,)), ((), ())),
+                preferred_element_type=f32) * (1.0 / math.sqrt(HEAD_SIZE))
+            scores = jnp.where(allowed, scores, -jnp.inf)
+            peak = jnp.max(scores, axis=1, keepdims=True)
+            weight = jnp.exp(scores - peak)
+            total_weight = jnp.sum(weight, axis=1, keepdims=True)
+            mixed = jnp.dot(weight.astype(bf16), value_rows, preferred_element_type=f32)
+            attn[span:keys, head * HEAD_SIZE:(head + 1) * HEAD_SIZE] = (
+                mixed / total_weight).astype(bf16)
+
+    tile = 256
+
+    loads[2].wait()
+    for i in range(4):
+        level = order[i]
+        span = pl.ds(pl.multiple_of(level * 2 * rows, 32), 2 * rows)
+        inputs = attn[span, :]
+
+        @pl.loop(0, width // tile)
+        def _(n):
+            cols = pl.ds(pl.multiple_of(n * tile, tile), tile)
+            out = jnp.dot(inputs, wo[:, cols], preferred_element_type=f32)
+            part[0, level, :, :, cols] = out.astype(bf16).reshape(2, rows, tile)
+
+        send_part(0, level).start()
+
+    attn_sum = scatter(0)
+    residual = (stream_ref[...].astype(f32) + attn_sum).astype(bf16)
+    resid[0] = residual.astype(f32)
+    gathered[1, t] = normed(resid[0], mlp_gain_ref).astype(bf16)
+
+    def fill_cache():
+        row = g * tokens + lax.broadcasted_iota(jnp.int32, (tokens, tokens), 0)
+        total = None
+        for k in range(4):
+            if k:
+                for copy in kv_copies(k):
+                    copy.wait()
+            pick = (slots_all[k, 0:1, :] == row).astype(f32).astype(bf16)
+            term = jnp.dot(pick, kv_all[k], preferred_element_type=f32)
+            total = term if total is None else total + term
+        cache_ref[...] = total.astype(bf16)
+        loads[3].wait()
+        loads[4].wait()
+        loads[5].wait()
+
+    hidden_width = wg.shape[1]
+
+    def feed_forward(level):
+        inputs = gathered[1, pl.ds(level * 2, 2)].reshape(2 * rows, width)
+        for start in range(0, hidden_width, tile):
+            stop = min(start + tile, hidden_width)
+            gate = jnp.dot(inputs, wg[:, start:stop], preferred_element_type=f32)
+            upward = jnp.dot(inputs, wu[:, start:stop], preferred_element_type=f32)
+            hidden[:, start:stop] = (gate / (1.0 + jnp.exp(-gate)) * upward).astype(bf16)
+        inner = hidden[...]
+
+        @pl.loop(0, width // tile)
+        def _(n):
+            cols = pl.ds(pl.multiple_of(n * tile, tile), tile)
+            out = jnp.dot(inner, wd[:, cols], preferred_element_type=f32)
+            part[1, level, :, :, cols] = out.astype(bf16).reshape(2, rows, tile)
+
+        send_part(1, level).start()
+
+    gather(1, fill_cache, feed_forward)
+    mlp_sum = scatter(1)
+    layer_out = (resid[0] + mlp_sum).astype(bf16)
+    layer_ref[...] = layer_out
+
+    slots = end_out.shape[1]
+    span_cols = end_out.shape[2]
+    row_id = t * rows + lax.broadcasted_iota(jnp.int32, (slots, rows), 1)
+    slot_id = lax.broadcasted_iota(jnp.int32, (slots, rows), 0)
+    end = jnp.int32(0)
+    hit = jnp.zeros((slots, rows), f32)
+    for k in range(lengths_ref.shape[1]):
+        end = end + lengths_ref[0, k]
+        hit = jnp.where((slot_id == k) & (row_id == end - 1), 1.0, hit)
+    terms = jnp.dot(hit.astype(bf16), layer_out, preferred_element_type=f32).astype(bf16)
+    for k in range(8):
+        first = k * 5 // 2 * 128
+        end_out[k] = terms[:, first:first + span_cols]
+
+    def end_copy(k):
+        peer = lax.rem(t + k, 8)
+        return pltpu.make_async_remote_copy(
+            src_ref=end_out.at[peer], dst_ref=end_in.at[k], send_sem=end_send.at[k],
+            recv_sem=end_recv.at[k], device_id=(g, peer), device_id_type=MESH)
+
+    for k in range(1, 8):
+        end_copy(k).start()
+    total = end_out[t].astype(f32)
+    for k in range(1, 8):
+        end_copy(k).wait()
+        total = total + end_in[k].astype(f32)
+    table[0] = total.astype(bf16)
+
+    def table_copy(k):
+        return pltpu.make_async_remote_copy(
+            src_ref=table.at[0], dst_ref=table.at[k], send_sem=table_send.at[k],
+            recv_sem=table_recv.at[k], device_id=(lax.rem(g + k, 4), t), device_id_type=MESH)
+
+    for k in range(1, 4):
+        table_copy(k).start()
+    prompts = lengths_ref.shape[1]
+    asked = request_ref[:, :slots]
+    column = lax.broadcasted_iota(jnp.int32, (asked.shape[0], slots), 1)
+    state = None
+    for k in range(4):
+        if k:
+            table_copy(k).wait()
+        batch = lax.rem(g + 4 - k, 4)
+        pick = ((asked == batch * prompts + column) & (column < prompts)).astype(f32).astype(bf16)
+        term = jnp.dot(pick, table[k], preferred_element_type=f32)
+        state = term if state is None else state + term
+    keep = state_ref.shape[1]
+    shifted = state[:, span_cols - keep:]
+    state_ref[...] = jnp.where(t % 2 == 1, shifted, state[:, :keep]).astype(bf16)
+
+
+def fused_device(
+    stream,
+    lengths,
+    page_table,
+    request_prompt,
+    attn_gain,
+    query_gain,
+    key_gain,
+    mlp_gain,
+    w_query,
+    key_value_weight,
+    w_out,
+    w_gate,
+    w_up,
+    w_down,
+):
+    rows, width = stream.shape
+    tokens = rows * 8
+    query_cols = w_query.shape[1]
+    keyval_cols = key_value_weight.shape[1]
+    hidden_width = w_gate.shape[1]
+    heads = query_cols // HEAD_SIZE
+    requests = request_prompt.shape[0]
+    state_cols = width // 8
+    half = HEAD_SIZE // 2
+    frequency = rope_base ** (-2.0 * jnp.arange(half, dtype=jnp.float32) / HEAD_SIZE)
+    frequency = jnp.concatenate([frequency, frequency])[None, :]
+    cache_rows = page_table[:, None] * PAGE_TOKENS + jnp.arange(PAGE_TOKENS, dtype=jnp.int32)[None, :]
+    slots = jnp.broadcast_to(cache_rows.reshape(1, tokens), (8, tokens))
+    asked = jnp.broadcast_to(request_prompt[:, None], (requests, 128))
+    bf16 = jnp.bfloat16
+    f32 = jnp.float32
+    vmem = pl.BlockSpec(memory_space=pltpu.VMEM)
+    smem = pl.BlockSpec(memory_space=pltpu.SMEM)
+    hbm = pl.BlockSpec(memory_space=pl.ANY)
+    dma = pltpu.SemaphoreType.DMA
+    layer_out, cache, state = pl.pallas_call(
+        fused_kernel,
+        out_shape=(
+            jax.ShapeDtypeStruct((rows, width), bf16),
+            jax.ShapeDtypeStruct((tokens, keyval_cols), bf16),
+            jax.ShapeDtypeStruct((requests, state_cols), bf16),
+        ),
+        in_specs=[smem] + [vmem] * 8 + [hbm] * 6,
+        out_specs=(vmem, vmem, vmem),
+        scratch_shapes=[
+            pltpu.VMEM((width, query_cols), bf16),
+            pltpu.VMEM((width, keyval_cols), bf16),
+            pltpu.VMEM((query_cols, width), bf16),
+            pltpu.VMEM((width, hidden_width), bf16),
+            pltpu.VMEM((width, hidden_width), bf16),
+            pltpu.VMEM((hidden_width, width), bf16),
+            pltpu.VMEM((2, 8, rows, width), bf16),
+            pltpu.VMEM((heads, tokens, HEAD_SIZE), bf16),
+            pltpu.VMEM((4, tokens, keyval_cols), bf16),
+            pltpu.VMEM((4, 8, tokens), jnp.int32),
+            pltpu.VMEM((tokens, query_cols), bf16),
+            pltpu.VMEM((2 * rows, hidden_width), bf16),
+            pltpu.VMEM((2, 4, 2, rows, width), bf16),
+            pltpu.VMEM((2, 4, rows, width), bf16),
+            pltpu.VMEM((2, 4, rows, width), bf16),
+            pltpu.VMEM((2, 2, 4, rows, width), bf16),
+            pltpu.VMEM((tokens, HEAD_SIZE), f32),
+            pltpu.VMEM((tokens, HEAD_SIZE), f32),
+            pltpu.VMEM((tokens, HEAD_SIZE), jnp.int32),
+            pltpu.VMEM((2, rows, width), f32),
+            pltpu.VMEM((8, 16, 384), bf16),
+            pltpu.VMEM((8, 16, 384), bf16),
+            pltpu.VMEM((4, 16, 384), bf16),
+            dma((6,)),
+            dma((2, 8)),
+            dma((2, 2, 4)),
+            dma((2, 4)),
+            dma((2, 4)),
+            dma((2, 4)),
+            dma((2, 2, 4)),
+            dma((2, 4)),
+            dma((4,)),
+            dma((4,)),
+            dma((4,)),
+            dma((4,)),
+            dma((8,)),
+            dma((8,)),
+            dma((4,)),
+            dma((4,)),
+        ],
+        compiler_params=pltpu.CompilerParams(
+            collective_id=0, has_side_effects=True, vmem_limit_bytes=60 * 1024 * 1024
+        ),
+        name="fused_layer",
+    )(
+        lengths, stream, slots, asked, attn_gain[None, :], query_gain[None, :], key_gain[None, :],
+        mlp_gain[None, :], frequency, w_query, key_value_weight, w_out, w_gate, w_up, w_down,
+    )
+    return layer_out, cache.reshape(tokens // PAGE_TOKENS, PAGE_TOKENS, keyval_cols), state
+
+
 def solution(mesh):
     placed = (
         P(("dp", "tensor"), None),
@@ -213,8 +732,9 @@
         P(None, "tensor"),
         P("tensor", None),
     )
+    fused = mesh.shape["tensor"] == KEY_VALUE_HEADS and mesh.shape["dp"] == 4
     return jax.shard_map(
-        per_device,
+        fused_device if fused else per_device,
         mesh=mesh,
         in_specs=placed,
         out_specs=(P(("dp", "tensor"), None), P("dp", None, "tensor"), P("dp", "tensor")),

time: 366 us -> 165 us (0.45)
  waiting for transfers between devices: 268 us -> 0 us
  Pallas kernels: 0 us -> 134 us
  matrix products: 36 us -> 0 us
  other arithmetic: 20.5 us -> 1.34 us
  local copies, waits for them, and re-layouts: 14.1 us -> 28 us
  between operations: 14.1 us -> 0.65 us
  starting transfers between devices: 7.6 us -> 0 us
  blocking collectives: 5.2 us -> 0 us
    pallas_call x0 -> x1, Pallas kernels: none -> 134 us  [fused_device(): pl.pallas_call(fused_kernel, out_shape=(jax.ShapeDtypeStruct((rows, width...]
    reduce_scatter x2 -> x0, waiting for transfers between devices: 114 us -> none  [the longest x1 66.4 us: per_device(): lax.psum_scatter(jnp.dot(attn, w_out, preferred_element_type=jnp.float32)...]
    all_gather x2 -> x0, waiting for transfers between devices: 91.4 us -> none  [the longest x1 46.3 us: per_device(): lax.all_gather(row_norm(resid, mlp_gain).astype(jnp.bfloat16), 'tensor',...]
    unnamed x6 -> x0, waiting for transfers between devices: 58.7 us -> none
    dot_general x9 -> x0, matrix products: 36 us -> none  [the longest x1 13 us: per_device(): jnp.dot(hidden, w_down, preferred_element_type=jnp.float32)]
    unnamed x29 -> x5, local copies, waits for them, and re-layouts: 3.67 us -> 23.4 us
    all_to_all x2 -> x0, starting transfers between devices: 7.22 us -> none  [the longest x1 3.99 us: per_device(): lax.all_to_all(send_pages, 'dp', split_axis=0, concat_axis=0, tiled=True)]
    convert_element_type x9 -> x0, other arithmetic: 6.66 us -> none  [the longest x4 2.03 us: row_norm(): return inputs * scale * gain.astype(jnp.float32)]
  transfers between devices with their start and end apart: 7 -> 0, of which waited for: 6 -> 0; matrix products, arithmetic and copies ran while one was open for 5% -> 0% of each run, Pallas kernels for 0% -> 0%
where the time goes in v1:
time: 165 us; the launch traced here: 164 us
  Pallas kernels  134 us (81%)
  local copies, waits for them, and re-layouts  28 us (17%)
    pallas_call x1, Pallas kernels, fused_device(): pl.pallas_call(fused_kernel, out_shape=(jax.ShapeDtypeStruct((rows, width...  134 us
    unnamed x5, local copies, waits for them, and re-layouts  23.4 us

profile of v1, /device:TPU:0, one launch (start us, length us, event | category | flops | bytes accessed | tf_op | source)
XLA Modules:
  0.0 164.0 jit_solution(17124709085527058080)
XLA Ops:
  0.6 0.7 broadcast_multiply_fusion
  1.3 0.6 maximum_bitcast_fusion.frequency_ref
  1.9 1.3 broadcast_in_dim.29.request_ref
  3.2 1.3 broadcast_in_dim.30.attn_gain_ref
  4.5 1.3 broadcast_in_dim.33.mlp_gain_ref
  5.8 0.1 iota_add_fusion
  5.9 0.1 add.23
  6.0 0.6 broadcast_in_dim.28.slots_ref
  6.6 9.4 %copy.19.wg_hbm = bf16[2560,1216]{1,0:T(8,128)(2,1)} copy(bf16[2560,1216]{0,1:T(8,128)(2,1)} %param.25) | data formatting | bytes 12451840 | tf_op args[11]
  16.0 9.4 %copy.20.wu_hbm = bf16[2560,1216]{1,0:T(8,128)(2,1)} copy(bf16[2560,1216]{0,1:T(8,128)(2,1)} %param.26) | data formatting | bytes 12451840 | tf_op args[12]
  25.4 134.0 %fused_layer.1 = (bf16[48,2560]{1,0:T(8,128)(2,1)}, bf16[384,256]{1,0:T(8,128)(2,1)}, bf16[16,320]{1,0:T(8,128)(2,1)}) custom-call(s32[1,6]{1,0:T(1,128)} %lengths_ref.1, bf16[48,2560]{1,0:T(8,128)(2,1)} %stream_ref.1, s32[8,384]{1,0:T(8,128)} %broadcast_in_dim.28.slots_ref, s32[16,128]{1,0:T(8,128)} %broadcast_in_dim.29.request_ref, ...), custom_call_target="tpu_custom_call" | custom-call | tf_op jit(solution)/shard_map/fused_layer/pallas_call | solution.py:657
  159.5 1.7 %copy.24 = bf16[48,2560]{1,0:T(8,128)(2,1)} copy(bf16[48,2560]{1,0:T(8,128)(2,1)} %get-tuple-element.12) | data formatting | bytes 491520
  161.1 1.6 copy.25
  162.7 1.3 copy.26
  (1 shorter events, 0.0 us)

commit v2 on v1

--- a/solution.py
+++ b/solution.py
@@ -2,6 +2,7 @@
 
 import jax
 import jax.numpy as jnp
+import numpy as np
 from jax import lax
 from jax.experimental import pallas as pl
 from jax.experimental.pallas import tpu as pltpu
@@ -201,9 +202,9 @@
 
 def fused_kernel(
     lengths_ref,
+    page_ref,
+    request_ref,
     stream_ref,
-    slots_ref,
-    request_ref,
     attn_gain_ref,
     query_gain_ref,
     key_gain_ref,
@@ -299,7 +300,7 @@
             src_ref=source, dst_ref=target, send_sem=send, recv_sem=recv,
             device_id=(g, (z + step) * 2 + y), device_id_type=MESH)
 
-    def gather(phase, before, process):
+    def gather(phase, before, process, after):
         def up(s):
             slot = (z - s) * 2 + y
             return z_copy(gathered.at[phase, slot], gathered.at[phase, slot],
@@ -353,6 +354,8 @@
                     across(z + s).start()
 
                 groups(s - 1)
+                if s == 3:
+                    after()
             else:
                 pl.when(z < 3)(lambda: up(0).start())
                 pl.when(z > 0)(lambda: down(0).start())
@@ -368,66 +371,68 @@
     packed = 27 + 72 * z - 15 * (z * (z - 1) // 2) + 5 * (z * (z - 1) * (z - 2))
     order = [packed % 4, packed // 4 % 4, packed // 16 % 4, packed // 64]
 
-    def send_part(phase, level):
-        return y_copy(part.at[phase, level, 1 - y], y_in.at[phase, level],
-                      rs_ysend.at[phase, level], rs_yrecv.at[phase, level])
-
-    def flow(phase, level, direction, step):
-        return z_copy(z_out.at[phase, level], z_in.at[phase, direction, level],
-                      rs_zsend.at[phase, level], rs_zrecv.at[phase, direction, level], step)
-
-    def scatter(phase):
-        for i in range(3):
-            level = order[i]
-            send_part(phase, level).wait_recv()
-
-            @pl.when(level > z)
+    piece = 512
+    pieces = width // piece
+
+    def columns(p):
+        return pl.ds(pl.multiple_of(p * piece, piece), piece)
+
+    def send_part(phase, level, p):
+        return y_copy(part.at[phase, level, 1 - y, :, columns(p)],
+                      y_in.at[phase, level, :, columns(p)],
+                      rs_ysend.at[phase, level, p], rs_yrecv.at[phase, level, p])
+
+    def flow(phase, level, direction, step, p):
+        return z_copy(z_out.at[phase, level, :, columns(p)],
+                      z_in.at[phase, direction, level, :, columns(p)],
+                      rs_zsend.at[phase, level, p], rs_zrecv.at[phase, direction, level, p], step)
+
+    def forward(phase, level, p):
+        cols = columns(p)
+        send_part(phase, level, p).wait_recv()
+        z_out[phase, level, :, cols] = (
+            part[phase, level, y, :, cols].astype(f32) + y_in[phase, level, :, cols].astype(f32)
+        ).astype(bf16)
+
+        def onward(direction, step, inner):
+            @pl.when(inner)
             def _():
-                total = part[phase, level, y].astype(f32) + y_in[phase, level].astype(f32)
-
-                @pl.when(z > 0)
-                def _():
-                    flow(phase, level, 0, 1).wait_recv()
-                    z_out[phase, level] = (total + z_in[phase, 0, level].astype(f32)).astype(bf16)
-
-                @pl.when(z == 0)
-                def _():
-                    z_out[phase, level] = total.astype(bf16)
-
-                flow(phase, level, 0, 1).start()
-
-            @pl.when(level < z)
+                flow(phase, level, direction, step, p).wait_recv()
+                z_out[phase, level, :, cols] = (
+                    part[phase, level, y, :, cols].astype(f32)
+                    + y_in[phase, level, :, cols].astype(f32)
+                    + z_in[phase, direction, level, :, cols].astype(f32)
+                ).astype(bf16)
+
+            flow(phase, level, direction, step, p).start()
+
+        pl.when(level > z)(lambda: onward(0, 1, z > 0))
+        pl.when(level < z)(lambda: onward(1, -1, z < 3))
+
+    def collect(phase):
+        @pl.loop(0, pieces)
+        def _(p):
+            cols = columns(p)
+            send_part(phase, z, p).wait_recv()
+            resid[1, :, cols] = (
+                part[phase, z, y, :, cols].astype(f32) + y_in[phase, z, :, cols].astype(f32))
+
+            @pl.when(z > 0)
             def _():
-                total = part[phase, level, y].astype(f32) + y_in[phase, level].astype(f32)
-
-                @pl.when(z < 3)
-                def _():
-                    flow(phase, level, 1, -1).wait_recv()
-                    z_out[phase, level] = (total + z_in[phase, 1, level].astype(f32)).astype(bf16)
-
-                @pl.when(z == 3)
-                def _():
-                    z_out[phase, level] = total.astype(bf16)
-
-                flow(phase, level, 1, -1).start()
-
-        send_part(phase, z).wait_recv()
-        resid[1] = part[phase, z, y].astype(f32) + y_in[phase, z].astype(f32)
-
-        @pl.when(z > 0)
-        def _():
-            flow(phase, z, 0, 1).wait_recv()
-            resid[1] = resid[1] + z_in[phase, 0, z].astype(f32)
-
-        @pl.when(z < 3)
-        def _():
-            flow(phase, z, 1, -1).wait_recv()
-            resid[1] = resid[1] + z_in[phase, 1, z].astype(f32)
-
-        for level in range(4):
-            send_part(phase, level).wait_send()
-            pl.when(z != level)(lambda: flow(phase, level, 0, 1).wait_send())
-        return resid[1]
+                flow(phase, z, 0, 1, p).wait_recv()
+                resid[1, :, cols] = resid[1, :, cols] + z_in[phase, 0, z, :, cols].astype(f32)
+
+            @pl.when(z < 3)
+            def _():
+                flow(phase, z, 1, -1, p).wait_recv()
+                resid[1, :, cols] = resid[1, :, cols] + z_in[phase, 1, z, :, cols].astype(f32)
+
+    def sent(phase):
+        @pl.loop(0, pieces)
+        def _(p):
+            for level in range(4):
+                send_part(phase, level, p).wait_send()
+                pl.when(z != level)(lambda: flow(phase, level, 0, 1, p).wait_send())
 
     def angles():
         ids = lax.broadcasted_iota(jnp.int32, (tokens, HEAD_SIZE), 0)
@@ -443,7 +448,11 @@
         cosine[...] = jnp.cos(angle)
         signed = jnp.sin(angle)
         sine[...] = jnp.where(lane < HEAD_SIZE // 2, -signed, signed)
-        slots_all[0] = slots_ref[...]
+        token = lax.broadcasted_iota(jnp.int32, slots_all.shape[1:], 1)
+        slots = jnp.zeros(slots_all.shape[1:], jnp.int32)
+        for k in range(page_ref.shape[0]):
+            slots = jnp.where(token // PAGE_TOKENS == k, page_ref[k], slots)
+        slots_all[0] = slots * PAGE_TOKENS + token % PAGE_TOKENS
         loads[0].wait()
         loads[1].wait()
 
@@ -468,7 +477,7 @@
         kv_all[0, span, :HEAD_SIZE] = rotated(normed(key_head, key_gain_ref)).astype(bf16)
         kv_all[0, span, HEAD_SIZE:] = keyval[:, HEAD_SIZE:]
 
-    gather(0, angles, project)
+    gather(0, angles, project, lambda: None)
 
     def kv_copies(k):
         peer = (lax.rem(g + k, 4), t)
@@ -485,46 +494,45 @@
         for copy in kv_copies(k):
             copy.start()
 
-    block = 128
-    for q_block in range(tokens // block):
-        span = q_block * block
-        keys = span + block
-        row_id = span + lax.broadcasted_iota(jnp.int32, (block, keys), 0)
-        key_id = lax.broadcasted_iota(jnp.int32, (block, keys), 1)
-        first = jnp.concatenate([starts[span:keys, :]] * (keys // block), axis=1)
-        allowed = (key_id >= first) & (key_id <= row_id)
-        key_rows = kv_all[0, :keys, :HEAD_SIZE]
-        value_rows = kv_all[0, :keys, HEAD_SIZE:]
+    tile = 256
+    group_rows = 2 * rows
+    loads[2].wait()
+    for i in range(4):
+        level = order[i]
+        first_row = pl.multiple_of(level * group_rows, 32)
+        span = pl.ds(first_row, group_rows)
+        row_id = first_row + lax.broadcasted_iota(jnp.int32, (group_rows, tokens), 0)
+        key_id = lax.broadcasted_iota(jnp.int32, (group_rows, tokens), 1)
+        begin = jnp.concatenate([starts[span, :]] * (tokens // HEAD_SIZE), axis=1)
+        allowed = (key_id >= begin) & (key_id <= row_id)
         for head in range(heads):
             scores = lax.dot_general(
-                q_rot[head, span:keys, :], key_rows, (((1,), (1,)), ((), ())),
+                q_rot[head, span, :], kv_all[0, :, :HEAD_SIZE], (((1,), (1,)), ((), ())),
                 preferred_element_type=f32) * (1.0 / math.sqrt(HEAD_SIZE))
             scores = jnp.where(allowed, scores, -jnp.inf)
             peak = jnp.max(scores, axis=1, keepdims=True)
             weight = jnp.exp(scores - peak)
             total_weight = jnp.sum(weight, axis=1, keepdims=True)
-            mixed = jnp.dot(weight.astype(bf16), value_rows, preferred_element_type=f32)
-            attn[span:keys, head * HEAD_SIZE:(head + 1) * HEAD_SIZE] = (
-                mixed / total_weight).astype(bf16)
-
-    tile = 256
-
-    loads[2].wait()
-    for i in range(4):
-        level = order[i]
-        span = pl.ds(pl.multiple_of(level * 2 * rows, 32), 2 * rows)
-        inputs = attn[span, :]
-
-        @pl.loop(0, width // tile)
-        def _(n):
-            cols = pl.ds(pl.multiple_of(n * tile, tile), tile)
+            mixed = jnp.dot(
+                weight.astype(bf16), kv_all[0, :, HEAD_SIZE:], preferred_element_type=f32)
+            attn[:, head * HEAD_SIZE:(head + 1) * HEAD_SIZE] = (mixed / total_weight).astype(bf16)
+        inputs = attn[...]
+
+        @pl.loop(0, pieces)
+        def _(p):
+            cols = columns(p)
             out = jnp.dot(inputs, wo[:, cols], preferred_element_type=f32)
-            part[0, level, :, :, cols] = out.astype(bf16).reshape(2, rows, tile)
-
-        send_part(0, level).start()
-
-    attn_sum = scatter(0)
-    residual = (stream_ref[...].astype(f32) + attn_sum).astype(bf16)
+            part[0, level, :, :, cols] = out.astype(bf16).reshape(2, rows, piece)
+            send_part(0, level, p).start()
+
+    for i in range(3):
+
+        @pl.loop(0, pieces)
+        def _(p):
+            forward(0, order[i], p)
+
+    collect(0)
+    residual = (stream_ref[...].astype(f32) + resid[1]).astype(bf16)
     resid[0] = residual.astype(f32)
     gathered[1, t] = normed(resid[0], mlp_gain_ref).astype(bf16)
 
@@ -543,28 +551,58 @@
         loads[4].wait()
         loads[5].wait()
 
-    hidden_width = wg.shape[1]
+    hidden_width = wg.shape[0]
+
+    across_cols = (((1,), (1,)), ((), ()))
 
     def feed_forward(level):
         inputs = gathered[1, pl.ds(level * 2, 2)].reshape(2 * rows, width)
         for start in range(0, hidden_width, tile):
             stop = min(start + tile, hidden_width)
-            gate = jnp.dot(inputs, wg[:, start:stop], preferred_element_type=f32)
-            upward = jnp.dot(inputs, wu[:, start:stop], preferred_element_type=f32)
+            gate = lax.dot_general(inputs, wg[start:stop, :], across_cols, preferred_element_type=f32)
+            upward = lax.dot_general(inputs, wu[start:stop, :], across_cols, preferred_element_type=f32)
             hidden[:, start:stop] = (gate / (1.0 + jnp.exp(-gate)) * upward).astype(bf16)
         inner = hidden[...]
 
-        @pl.loop(0, width // tile)
-        def _(n):
-            cols = pl.ds(pl.multiple_of(n * tile, tile), tile)
+        @pl.loop(0, pieces)
+        def _(p):
+            cols = columns(p)
             out = jnp.dot(inner, wd[:, cols], preferred_element_type=f32)
-            part[1, level, :, :, cols] = out.astype(bf16).reshape(2, rows, tile)
-
-        send_part(1, level).start()
-
-    gather(1, fill_cache, feed_forward)
-    mlp_sum = scatter(1)
-    layer_out = (resid[0] + mlp_sum).astype(bf16)
+            part[1, level, :, :, cols] = out.astype(bf16).reshape(2, rows, piece)
+            send_part(1, level, p).start()
+
+    outer = (z == 0) | (z == 3)
+
+    def early():
+        @pl.when(outer)
+        def _():
+            @pl.loop(0, pieces)
+            def _(p):
+                forward(1, order[2], p)
+
+    gather(1, fill_cache, feed_forward, early)
+
+    @pl.when(outer)
+    def _():
+        for i in (1, 0):
+
+            @pl.loop(0, pieces)
+            def _(p):
+                forward(1, order[i], p)
+
+    @pl.when(jnp.logical_not(outer))
+    def _():
+        @pl.loop(0, pieces)
+        def _(p):
+            forward(1, order[2], p)
+
+        @pl.loop(0, pieces)
+        def _(p):
+            forward(1, order[0], p)
+            forward(1, order[1], p)
+
+    collect(1)
+    layer_out = (resid[0] + resid[1]).astype(bf16)
     layer_ref[...] = layer_out
 
     slots = end_out.shape[1]
@@ -603,8 +641,12 @@
     for k in range(1, 4):
         table_copy(k).start()
     prompts = lengths_ref.shape[1]
-    asked = request_ref[:, :slots]
-    column = lax.broadcasted_iota(jnp.int32, (asked.shape[0], slots), 1)
+    requests = request_ref.shape[0]
+    line = lax.broadcasted_iota(jnp.int32, (requests, slots), 0)
+    column = lax.broadcasted_iota(jnp.int32, (requests, slots), 1)
+    asked = jnp.zeros((requests, slots), jnp.int32)
+    for k in range(requests):
+        asked = jnp.where(line == k, request_ref[k], asked)
     state = None
     for k in range(4):
         if k:
@@ -613,6 +655,8 @@
         pick = ((asked == batch * prompts + column) & (column < prompts)).astype(f32).astype(bf16)
         term = jnp.dot(pick, table[k], preferred_element_type=f32)
         state = term if state is None else state + term
+    sent(0)
+    sent(1)
     keep = state_ref.shape[1]
     shifted = state[:, span_cols - keep:]
     state_ref[...] = jnp.where(t % 2 == 1, shifted, state[:, :keep]).astype(bf16)
@@ -642,12 +686,9 @@
     heads = query_cols // HEAD_SIZE
     requests = request_prompt.shape[0]
     state_cols = width // 8
-    half = HEAD_SIZE // 2
-    frequency = rope_base ** (-2.0 * jnp.arange(half, dtype=jnp.float32) / HEAD_SIZE)
-    frequency = jnp.concatenate([frequency, frequency])[None, :]
-    cache_rows = page_table[:, None] * PAGE_TOKENS + jnp.arange(PAGE_TOKENS, dtype=jnp.int32)[None, :]
-    slots = jnp.broadcast_to(cache_rows.reshape(1, tokens), (8, tokens))
-    asked = jnp.broadcast_to(request_prompt[:, None], (requests, 128))
+    pieces = width // 512
+    exponents = -2.0 * (np.arange(HEAD_SIZE) % (HEAD_SIZE // 2)) / HEAD_SIZE
+    frequency = np.power(rope_base, exponents).astype(np.float32)[None, :]
     bf16 = jnp.bfloat16
     f32 = jnp.float32
     vmem = pl.BlockSpec(memory_space=pltpu.VMEM)
@@ -661,20 +702,20 @@
             jax.ShapeDtypeStruct((tokens, keyval_cols), bf16),
             jax.ShapeDtypeStruct((requests, state_cols), bf16),
         ),
-        in_specs=[smem] + [vmem] * 8 + [hbm] * 6,
+        in_specs=[smem] * 3 + [vmem] * 6 + [hbm] * 6,
         out_specs=(vmem, vmem, vmem),
         scratch_shapes=[
             pltpu.VMEM((width, query_cols), bf16),
             pltpu.VMEM((width, keyval_cols), bf16),
             pltpu.VMEM((query_cols, width), bf16),
-            pltpu.VMEM((width, hidden_width), bf16),
-            pltpu.VMEM((width, hidden_width), bf16),
+            pltpu.VMEM((hidden_width, width), bf16),
+            pltpu.VMEM((hidden_width, width), bf16),
             pltpu.VMEM((hidden_width, width), bf16),
             pltpu.VMEM((2, 8, rows, width), bf16),
             pltpu.VMEM((heads, tokens, HEAD_SIZE), bf16),
             pltpu.VMEM((4, tokens, keyval_cols), bf16),
             pltpu.VMEM((4, 8, tokens), jnp.int32),
-            pltpu.VMEM((tokens, query_cols), bf16),
+            pltpu.VMEM((2 * rows, query_cols), bf16),
             pltpu.VMEM((2 * rows, hidden_width), bf16),
             pltpu.VMEM((2, 4, 2, rows, width), bf16),
             pltpu.VMEM((2, 4, rows, width), bf16),
@@ -691,10 +732,10 @@
             dma((2, 8)),
             dma((2, 2, 4)),
             dma((2, 4)),
-            dma((2, 4)),
-            dma((2, 4)),
-            dma((2, 2, 4)),
-            dma((2, 4)),
+            dma((2, 4, pieces)),
+            dma((2, 4, pieces)),
+            dma((2, 2, 4, pieces)),
+            dma((2, 4, pieces)),
             dma((4,)),
             dma((4,)),
             dma((4,)),
@@ -709,8 +750,8 @@
         ),
         name="fused_layer",
     )(
-        lengths, stream, slots, asked, attn_gain[None, :], query_gain[None, :], key_gain[None, :],
-        mlp_gain[None, :], frequency, w_query, key_value_weight, w_out, w_gate, w_up, w_down,
+        lengths, page_table, request_prompt, stream, attn_gain[None, :], query_gain[None, :], key_gain[None, :],
+        mlp_gain[None, :], frequency, w_query, key_value_weight, w_out, w_gate.T, w_up.T, w_down,
     )
     return layer_out, cache.reshape(tokens // PAGE_TOKENS, PAGE_TOKENS, keyval_cols), state
 

time: 165 us -> 144 us (0.87)
  local copies, waits for them, and re-layouts: 28 us -> 7.17 us
  Pallas kernels: 134 us -> 136 us
    unnamed x5 -> x3, local copies, waits for them, and re-layouts: 23.4 us -> 4.58 us
    broadcast_in_dim x2 -> x0, local copies, waits for them, and re-layouts: 1.92 us -> none  [the longest x1 1.31 us: fused_device(): asked = jnp.broadcast_to(request_prompt[:, None], (requests, 128))]
    pallas_call x1, Pallas kernels: 134 us -> 136 us  [fused_device(): pl.pallas_call(fused_kernel, out_shape=(jax.ShapeDtypeStruct((rows, width...]
where the time goes in v2:
time: 144 us
  Pallas kernels  136 us (94%)
  local copies, waits for them, and re-layouts  7.17 us (5%)
    pallas_call x1, Pallas kernels, fused_device(): pl.pallas_call(fused_kernel, out_shape=(jax.ShapeDtypeStruct((rows, width...  136 us
    unnamed x3, local copies, waits for them, and re-layouts  4.58 us

profile of v2, /device:TPU:0, one launch (start us, length us, event | category | flops | bytes accessed | tf_op | source)
XLA Modules:
  0.0 143.8 jit_solution(18241970778303402566)
XLA Ops:
  0.6 1.3 broadcast_in_dim.12.attn_gain_ref
  1.9 1.3 broadcast_in_dim.15.mlp_gain_ref
  3.2 135.9 %fused_layer.1 = (bf16[48,2560]{1,0:T(8,128)(2,1)}, bf16[384,256]{1,0:T(8,128)(2,1)}, bf16[16,320]{1,0:T(8,128)(2,1)}) custom-call(s32[1,6]{1,0:T(1,128)} %lengths_ref.1, s32[24]{0:T(128)} %page_ref.1, s32[16]{0:T(128)} %request_ref.1, bf16[48,2560]{1,0:T(8,128)(2,1)} %stream_ref.1, bf16[1,2560]{1,0:T(2,128)(2,1)} %broadcast_in_dim.12.attn_gain_ref, ...), custom_call_target="tpu_custom_call" | custom-call | tf_op jit(solution)/shard_map/fused_layer/pallas_call | solution.py:698
  139.2 1.7 %copy.21 = bf16[48,2560]{1,0:T(8,128)(2,1)} copy(bf16[48,2560]{1,0:T(8,128)(2,1)} %get-tuple-element.12) | data formatting | bytes 491520
  140.8 1.6 %copy.22 = bf16[24,16,256]{2,1,0:T(8,128)(2,1)} copy(bf16[24,16,256]{2,1,0:T(8,128)(2,1)} %bitcast.7) | data formatting | bytes 393216
  142.5 1.3 copy.23

commit v3 on v2

--- a/solution.py
+++ b/solution.py
@@ -285,7 +285,8 @@
 
     def normed(value, gain_ref):
         scale = lax.rsqrt(jnp.mean(value * value, axis=-1, keepdims=True) + epsilon)
-        return value * scale * gain_ref[...].astype(f32)
+        gain = gain_ref[...].astype(f32)
+        return value * scale * (gain.reshape(1, -1) if gain.ndim == 1 else gain)
 
     gathered[0, t] = normed(stream_ref[...].astype(f32), attn_gain_ref).astype(bf16)
     pl.semaphore_wait(barrier, 10)
@@ -378,30 +379,29 @@
         return pl.ds(pl.multiple_of(p * piece, piece), piece)
 
     def send_part(phase, level, p):
-        return y_copy(part.at[phase, level, 1 - y, :, columns(p)],
-                      y_in.at[phase, level, :, columns(p)],
+        return y_copy(part.at[phase, level, 1 - y, p],
+                      y_in.at[phase, level, p],
                       rs_ysend.at[phase, level, p], rs_yrecv.at[phase, level, p])
 
     def flow(phase, level, direction, step, p):
-        return z_copy(z_out.at[phase, level, :, columns(p)],
-                      z_in.at[phase, direction, level, :, columns(p)],
+        return z_copy(z_out.at[phase, level, p],
+                      z_in.at[phase, direction, level, p],
                       rs_zsend.at[phase, level, p], rs_zrecv.at[phase, direction, level, p], step)
 
     def forward(phase, level, p):
-        cols = columns(p)
         send_part(phase, level, p).wait_recv()
-        z_out[phase, level, :, cols] = (
-            part[phase, level, y, :, cols].astype(f32) + y_in[phase, level, :, cols].astype(f32)
+        z_out[phase, level, p] = (
+            part[phase, level, y, p].astype(f32) + y_in[phase, level, p].astype(f32)
         ).astype(bf16)
 
         def onward(direction, step, inner):
             @pl.when(inner)
             def _():
                 flow(phase, level, direction, step, p).wait_recv()
-                z_out[phase, level, :, cols] = (
-                    part[phase, level, y, :, cols].astype(f32)
-                    + y_in[phase, level, :, cols].astype(f32)
-                    + z_in[phase, direction, level, :, cols].astype(f32)
+                z_out[phase, level, p] = (
+                    part[phase, level, y, p].astype(f32)
+                    + y_in[phase, level, p].astype(f32)
+                    + z_in[phase, direction, level, p].astype(f32)
                 ).astype(bf16)
 
             flow(phase, level, direction, step, p).start()
@@ -415,17 +415,17 @@
             cols = columns(p)
             send_part(phase, z, p).wait_recv()
             resid[1, :, cols] = (
-                part[phase, z, y, :, cols].astype(f32) + y_in[phase, z, :, cols].astype(f32))
+                part[phase, z, y, p].astype(f32) + y_in[phase, z, p].astype(f32))
 
             @pl.when(z > 0)
             def _():
                 flow(phase, z, 0, 1, p).wait_recv()
-                resid[1, :, cols] = resid[1, :, cols] + z_in[phase, 0, z, :, cols].astype(f32)
+                resid[1, :, cols] = resid[1, :, cols] + z_in[phase, 0, z, p].astype(f32)
 
             @pl.when(z < 3)
             def _():
                 flow(phase, z, 1, -1, p).wait_recv()
-                resid[1, :, cols] = resid[1, :, cols] + z_in[phase, 1, z, :, cols].astype(f32)
+                resid[1, :, cols] = resid[1, :, cols] + z_in[phase, 1, z, p].astype(f32)
 
     def sent(phase):
         @pl.loop(0, pieces)
@@ -493,6 +493,8 @@
     for k in range(1, 4):
         for copy in kv_copies(k):
             copy.start()
+
+    outer = (z == 0) | (z == 3)
 
     tile = 256
     group_rows = 2 * rows
@@ -522,14 +524,20 @@
         def _(p):
             cols = columns(p)
             out = jnp.dot(inputs, wo[:, cols], preferred_element_type=f32)
-            part[0, level, :, :, cols] = out.astype(bf16).reshape(2, rows, piece)
+            part[0, level, :, p] = out.astype(bf16).reshape(2, rows, piece)
             send_part(0, level, p).start()
 
-    for i in range(3):
-
-        @pl.loop(0, pieces)
-        def _(p):
-            forward(0, order[i], p)
+        def pass_on(k):
+            @pl.loop(0, pieces)
+            def _(p):
+                forward(0, order[k], p)
+
+        if i >= 1:
+            pl.when(outer)(lambda: pass_on(i - 1))
+        if i >= 2:
+            pl.when(jnp.logical_not(outer))(lambda: pass_on(i - 2))
+        if i == 3:
+            pl.when(jnp.logical_not(outer))(lambda: pass_on(2))
 
     collect(0)
     residual = (stream_ref[...].astype(f32) + resid[1]).astype(bf16)
@@ -568,10 +576,8 @@
         def _(p):
             cols = columns(p)
             out = jnp.dot(inner, wd[:, cols], preferred_element_type=f32)
-            part[1, level, :, :, cols] = out.astype(bf16).reshape(2, rows, piece)
+            part[1, level, :, p] = out.astype(bf16).reshape(2, rows, piece)
             send_part(1, level, p).start()
-
-    outer = (z == 0) | (z == 3)
 
     def early():
         @pl.when(outer)
@@ -717,10 +723,10 @@
             pltpu.VMEM((4, 8, tokens), jnp.int32),
             pltpu.VMEM((2 * rows, query_cols), bf16),
             pltpu.VMEM((2 * rows, hidden_width), bf16),
-            pltpu.VMEM((2, 4, 2, rows, width), bf16),
-            pltpu.VMEM((2, 4, rows, width), bf16),
-            pltpu.VMEM((2, 4, rows, width), bf16),
-            pltpu.VMEM((2, 2, 4, rows, width), bf16),
+            pltpu.VMEM((2, 4, 2, pieces, rows, 512), bf16),
+            pltpu.VMEM((2, 4, pieces, rows, 512), bf16),
+            pltpu.VMEM((2, 4, pieces, rows, 512), bf16),
+            pltpu.VMEM((2, 2, 4, pieces, rows, 512), bf16),
             pltpu.VMEM((tokens, HEAD_SIZE), f32),
             pltpu.VMEM((tokens, HEAD_SIZE), f32),
             pltpu.VMEM((tokens, HEAD_SIZE), jnp.int32),
@@ -750,8 +756,8 @@
         ),
         name="fused_layer",
     )(
-        lengths, page_table, request_prompt, stream, attn_gain[None, :], query_gain[None, :], key_gain[None, :],
-        mlp_gain[None, :], frequency, w_query, key_value_weight, w_out, w_gate.T, w_up.T, w_down,
+        lengths, page_table, request_prompt, stream, attn_gain, query_gain[None, :], key_gain[None, :],
+        mlp_gain, frequency, w_query, key_value_weight, w_out, w_gate.T, w_up.T, w_down,
     )
     return layer_out, cache.reshape(tokens // PAGE_TOKENS, PAGE_TOKENS, keyval_cols), state
 

time: 144 us -> 139 us (0.965)
  local copies, waits for them, and re-layouts: 7.17 us -> 4.58 us
  Pallas kernels: 136 us -> 134 us
    broadcast_in_dim x2 -> x0, local copies, waits for them, and re-layouts: 2.59 us -> none  [the longest x1 1.3 us: fused_device(): attn_gain[None, :]]
    pallas_call x1, Pallas kernels: 136 us -> 134 us  [fused_device(): pl.pallas_call(fused_kernel, out_shape=(jax.ShapeDtypeStruct((rows, width...]
where the time goes in v3:
time: 139 us
  Pallas kernels  134 us (96%)
  local copies, waits for them, and re-layouts  4.58 us (3%)
    pallas_call x1, Pallas kernels, fused_device(): pl.pallas_call(fused_kernel, out_shape=(jax.ShapeDtypeStruct((rows, width...  134 us
    unnamed x3, local copies, waits for them, and re-layouts  4.58 us

profile of v3, /device:TPU:0, one launch (start us, length us, event | category | flops | bytes accessed | tf_op | source)
XLA Modules:
  0.0 138.8 jit_solution(6481116613325207283)
XLA Ops:
  0.6 133.6 %fused_layer.1 = (bf16[48,2560]{1,0:T(8,128)(2,1)}, bf16[384,256]{1,0:T(8,128)(2,1)}, bf16[16,320]{1,0:T(8,128)(2,1)}) custom-call(s32[1,6]{1,0:T(1,128)} %lengths_ref.1, s32[24]{0:T(128)} %page_ref.1, s32[16]{0:T(128)} %request_ref.1, bf16[48,2560]{1,0:T(8,128)(2,1)} %stream_ref.1, bf16[2560]{0:T(1024)(128)(2,1)} %attn_gain_ref.1, bf16[1,128]{1,0:T(2,128)(2,1)} %bitcast.8, ...), custom_call_target="tpu_custom_call" | custom-call | tf_op jit(solution)/shard_map/fused_layer/pallas_call | solution.py:704
  134.2 1.7 %copy.21 = bf16[48,2560]{1,0:T(8,128)(2,1)} copy(bf16[48,2560]{1,0:T(8,128)(2,1)} %get-tuple-element.12) | data formatting | bytes 491520
  135.9 1.6 %copy.22 = bf16[24,16,256]{2,1,0:T(8,128)(2,1)} copy(bf16[24,16,256]{2,1,0:T(8,128)(2,1)} %bitcast.7) | data formatting | bytes 393216
  137.5 1.3 copy.23
